TPU v7x, 32 devices: a whole 2x2x4 slice. The times are simulated.
32 devices in a mesh: users: 16 (over z, y, core), items: 2 (over x).
Axes of the slice: x: 2, y: 2, z: 4, core: 2. Of those that a mesh axis runs over, the one named last changes fastest.
Arguments:
- interactions: bfloat16 [3, 20480, 512], P(None, 'users', 'items')
- matchings: int32 [3], replicated, may hold values from 1 to 15, as said below
- user_shape: bfloat16 [20480, 128], P('users'), may hold values from 0.5 to 2
- item_shape: bfloat16 [8192, 128], P(('users', 'items')), may hold values from 0.5 to 2
Outputs:
- user_log: bfloat16 [20480, 128], P('users')
- item_log: bfloat16 [8192, 128], P(('users', 'items'))
Inputs may be any that keep to these rules, and one draw needn't show every extreme that they name: matchings[0] and matchings[1] are two different values of 1 to 14, and the last matching is 15.
All inputs are finite; a program needn't handle non-finite values.
Results may differ from a plain program's by a relative error of at most 0.0012.
The roundings to bfloat16 on the way count: a program that leaves them out, or rounds other values in their place, can miss the bound.
Values sent between devices are 32-bit elements; how exact they have to be, the bound alone decides.
No kernel may reach another device: no remote copies, remote signals or barrier semaphores. Data moves between devices by JAX's collectives and lax.ppermute only.
A program may use at most 64 MiB of HBM per device.

v0:
```python
import functools

import jax
import jax.numpy as jnp
from jax import lax
from jax.experimental import pallas as pl
from jax.experimental.pallas import tpu as pltpu
from jax.sharding import PartitionSpec as P

STRATA = 3
TILE = 64
START_TILE = 128
F32 = jnp.float32
BF16 = jnp.bfloat16


def chunk_rows(rows):
    first = max(rows // 2 // TILE, 1) * TILE
    return [first, rows - first] if first < rows else [rows]


def tail_rows(rows):
    return rows // 2 // TILE * TILE


def psi_parts(x):
    small = x < 8.0
    w = jnp.where(small, x + 3.5, x - 0.5)
    q = x * (x + 3.0)
    q2 = q + 2.0
    bounded = jnp.minimum(w, 1e9)
    square = bounded * bounded
    steps = jnp.where(small, q * q2, 1.0)
    r = 1.0 / (square * steps)
    s = r * steps
    shift = (2.0 * x + 3.0) * (q + q2) * (r * square)
    g = s * (1.0 / 24.0 - s * (7.0 / 960.0 - s * (31.0 / 8064.0 - s * (127.0 / 30720.0))))
    return w, g - jnp.where(small, shift, 0.0)


def psi_any(x):
    mirrored = x < 0.5
    w, g = psi_parts(jnp.where(mirrored, 1.0 - x, x))
    value = jnp.log(w) + g
    t = x - jnp.floor(x + 0.5)
    u = 3.14159265358979 * t
    v = u * u
    sin = 1.0 / 6227020800.0
    for c in (-1.0 / 39916800.0, 1.0 / 362880.0, -1.0 / 5040.0, 1.0 / 120.0, -1.0 / 6.0, 1.0):
        sin = sin * v + c
    cos = -1.0 / 87178291200.0
    for c in (1.0 / 479001600.0, -1.0 / 3628800.0, 1.0 / 40320.0, -1.0 / 720.0, 1.0 / 24.0, -0.5, 1.0):
        cos = cos * v + c
    value = jnp.where(mirrored, value - 3.14159265358979 * cos / (sin * u), value)
    return jnp.where((x <= 0.0) & (x == jnp.floor(x)), jnp.nan, value)


LOWEST = 0.01


def above(low):
    return jnp.min(low) >= LOWEST


def folded(x):
    return x.reshape(x.shape[0] // 8, 8, x.shape[1])


def tiles(rows):
    step = TILE if rows % TILE == 0 else rows
    return [(at, step) for at in range(0, rows, step)]


def exp_tile(x, rte, general):
    shape = x.shape
    x = folded(x)
    if general:
        value = psi_any(x)
        if rte is not None:
            value = value - jnp.log(rte)[None]
        value = jnp.exp(value)
    else:
        w, g = psi_parts(x)
        value = w if rte is None else w * (1.0 / rte)[None]
        value = value * jnp.exp(g)
    mean = x if rte is None else x * (1.0 / rte)[None]
    return value.reshape(shape).astype(BF16), jnp.sum(mean, axis=0), jnp.min(x, axis=0)


def log_tile(x, rte, general):
    shape = x.shape
    x = folded(x)
    if general:
        value = psi_any(x) - jnp.log(rte)[None]
    else:
        w, g = psi_parts(x)
        value = (jnp.log(w) - jnp.log(rte)[None]) + g
    return value.reshape(shape).astype(BF16), jnp.min(x, axis=0)


def row_sum(x):
    return jnp.broadcast_to(jnp.sum(x, axis=0, keepdims=True), x.shape)


VMEM_SPEC = pl.BlockSpec(memory_space=pltpu.VMEM)
SMEM_SPEC = pl.BlockSpec(memory_space=pltpu.SMEM)
HBM_SPEC = pl.BlockSpec(memory_space=pltpu.HBM)
PARAMS = pltpu.CompilerParams(vmem_limit_bytes=24 * 2**20)


def in_hbm(x):
    return pltpu.with_memory_space_constraint(x, pltpu.HBM)


def in_vmem(x):
    return pltpu.with_memory_space_constraint(x, pltpu.VMEM)


def prepare_kernel(matchings_hbm, shape_hbm, item, *refs, last):
    choices, (matchings, shape, sems) = refs[:STRATA], refs[STRATA:]
    copies = [
        pltpu.make_async_copy(shape_hbm, shape, sems.at[0]),
        pltpu.make_async_copy(matchings_hbm, matchings, sems.at[1]),
    ]
    for copy in copies:
        copy.start()
    for copy in copies:
        copy.wait()
    item[...] = shape[...].astype(F32)
    choices[0][0] = matchings[0] - 1
    for stratum in range(1, STRATA - 1):
        choices[stratum][0] = jnp.bitwise_xor(matchings[stratum - 1], matchings[stratum]) - 1
    choices[STRATA - 1][0] = jnp.bitwise_xor(matchings[STRATA - 2], last) - 1


def prepare_call(matchings, item_shape, last):
    out = pl.pallas_call(
        functools.partial(prepare_kernel, last=last),
        out_shape=[jax.ShapeDtypeStruct(item_shape.shape, F32)]
        + [pltpu.SMEM((1,), jnp.int32)] * STRATA,
        in_specs=[HBM_SPEC, HBM_SPEC],
        out_specs=[VMEM_SPEC] + [SMEM_SPEC] * STRATA,
        scratch_shapes=[pltpu.SMEM(matchings.shape, jnp.int32), pltpu.VMEM(item_shape.shape, BF16),
                        pltpu.SemaphoreType.DMA((2,))],
        compiler_params=PARAMS,
        name="prepare",
    )(in_hbm(matchings), in_hbm(item_shape))
    return out[0], [choice[0] for choice in out[1:]]


def start_kernel(shape_hbm, interactions, uexp, theta, counts, shape, sems):
    rows, depth = shape.shape
    load = pltpu.make_async_copy(shape_hbm, shape, sems.at[0])
    ahead = pltpu.make_async_copy(interactions.at[0, pl.ds(0, counts.shape[0]), :], counts, sems.at[1])
    load.start()
    ahead.start()
    load.wait()

    def body(general):
        def step(i, carry):
            total, low = carry
            place = pl.ds(pl.multiple_of(i * START_TILE, START_TILE), START_TILE)
            value, part, part_low = exp_tile(shape[place, :].astype(F32), None, general)
            uexp[place, :] = value
            return total + part, jnp.minimum(low, part_low)

        total, low = lax.fori_loop(
            0, rows // START_TILE, step, (jnp.zeros((8, depth), F32), jnp.ones((8, depth), F32)))
        theta[...] = total
        return low

    low = body(False)

    @pl.when(jnp.logical_not(above(low)))
    def _():
        body(True)

    ahead.wait()


def start_call(user_shape, interactions, first_rows):
    rows, depth = user_shape.shape
    items = interactions.shape[2]
    return pl.pallas_call(
        start_kernel,
        out_shape=[pltpu.VMEM((rows, depth), BF16), pltpu.VMEM((8, depth), F32),
                   pltpu.VMEM((first_rows, items), BF16)],
        in_specs=[HBM_SPEC] * 2,
        out_specs=[VMEM_SPEC] * 3,
        scratch_shapes=[pltpu.VMEM((rows, depth), BF16), pltpu.SemaphoreType.DMA((2,))],
        compiler_params=PARAMS,
        cost_estimate=pl.CostEstimate(
            flops=40 * rows * depth, bytes_accessed=rows * depth * 4, transcendentals=2 * rows * depth),
        name="user_start",
    )(in_hbm(user_shape), in_hbm(interactions))


def stratum_kernel(names, *refs, stratum, at, rows, items, factor, first, last, tail, ahead):
    ref = dict(zip(names, refs))
    copies = {}

    def fetch(name, source, target):
        copies[name] = pltpu.make_async_copy(source, target, ref["sems"].at[len(copies)])
        copies[name].start()

    if "item_in" in ref:
        fetch("item", ref["item"], ref["item_in"])
    if ahead:
        fetch("ahead", ref["interactions"].at[ahead[0], pl.ds(ahead[1], ahead[2]), :], ref["counts_ahead"])
    upart, counts, ratios, denominator = ref["upart"], ref["counts"], ref["ratios"], ref["denominator"]
    uexp = ref["uexp_all"].at[pl.ds(at, rows), :] if stratum == 0 else ref["uexp"]
    extra = 8 if first else 0

    def wait(name, general):
        if name in copies and not general:
            copies[name].wait()

    def body(general):
        lows = []
        theta = None
        if stratum > 0:
            if first:
                beta = row_sum(ref["acc"][0:8, :] + ref["recv"][0:8, :])
                old = 1.0 if stratum == 1 else ref["rte_old"][...]
                rte = 0.5 * old + 0.5 * (0.3 + factor * beta)
                ref["rte_new"][...] = rte
            else:
                rte = ref["rte"][...]
            lows.append(rte)
            for t, step in tiles(rows):
                old = ref["user_shape"][at + t:at + t + step, :].astype(F32) if stratum == 1 else ref["shp_old"][t:t + step, :]
                stat = ref["acc"][extra + t:extra + t + step, :] + ref["recv"][extra + t:extra + t + step, :]
                shp = 0.5 * old + 0.5 * (0.3 + factor * stat)
                ref["shp_new"][t:t + step, :] = shp
                value, part, low = exp_tile(shp, rte, general)
                uexp[t:t + step, :] = value
                theta = part if theta is None else theta + part
                lows.append(low)
            if not first:
                theta = theta + ref["theta"][...]
        elif last:
            theta = ref["theta"][...]

        if first:
            wait("item", general)
            item = ref["item_in"] if "item_in" in ref else ref["item"]
            if not last:
                ref["item_kept"][...] = item[...]
        elif last:
            item = ref["item_kept"]
        if first or last:
            item_rte = None if stratum == 0 else item[items:items + 8, :]
        if first:
            value, sums, low = exp_tile(item[0:items, :], item_rte, general)
            ref["item_exp_new"][...] = value
            upart[0:8, :] = sums
            lows.append(low)
            if item_rte is not None:
                lows.append(item_rte)
            item_exp = value
        else:
            item_exp = ref["item_exp"][...]

        denominator[...] = lax.dot_general(
            uexp[...], item_exp, (((1,), (1,)), ((), ())), preferred_element_type=F32)
        for t, step in tiles(rows):
            ratios[t:t + step, :] = (
                counts[t:t + step, :].astype(F32) / denominator[t:t + step, :]).astype(BF16)
        user_sums = uexp[...].astype(F32) * jnp.dot(
            ratios[...], item_exp, preferred_element_type=F32)
        upart[extra:extra + rows - tail, :] = user_sums[0:rows - tail, :]
        if tail:
            ref["upart_tail"][...] = user_sums[rows - tail:, :]
        istat = lax.dot_general(ratios[...], uexp[...], (((0,), (0,)), ((), ())), preferred_element_type=F32)
        if not first:
            istat = istat + ref["istat"][...]
        if last:
            old = 1.0 if item_rte is None else item_rte
            ref["item_new"][0:items, :] = 0.5 * item[0:items, :] + 0.5 * (
                0.3 + factor * (item_exp.astype(F32) * istat))
            ref["item_new"][items:items + 8, :] = 0.5 * old + 0.5 * (0.3 + factor * row_sum(theta))
        else:
            ref["istat_new"][...] = istat
            if stratum > 0:
                ref["theta_new"][...] = theta
        return functools.reduce(jnp.minimum, lows) if lows else None

    low = body(False)
    if low is not None:

        @pl.when(jnp.logical_not(above(low)))
        def _():
            body(True)

    wait("ahead", False)


def stratum_call(stratum, at, rows, items, depth, factor, first, last, tail, ahead, operands):
    extra = 8 if first else 0
    outs = {"upart": ((rows + extra - tail, depth), F32)}
    if tail:
        outs["upart_tail"] = ((tail, depth), F32)
    if stratum > 0:
        outs["shp_new"] = ((rows, depth), F32)
    if first and stratum > 0:
        outs["rte_new"] = ((8, depth), F32)
    if first:
        outs["item_exp_new"] = ((items, depth), BF16)
    if first and not last:
        outs["item_kept"] = (operands["item"].shape, F32)
    if last:
        outs["item_new"] = ((items + 8, depth), F32)
    else:
        outs["istat_new"] = ((items, depth), F32)
        if stratum > 0:
            outs["theta_new"] = ((8, depth), F32)
    if ahead:
        outs["counts_ahead"] = ((ahead[2], items), BF16)
    scratch = {
        "ratios": pltpu.VMEM((rows, items), BF16),
        "denominator": pltpu.VMEM((rows, items), F32),
        "sems": pltpu.SemaphoreType.DMA((2,)),
    }
    if stratum > 0:
        scratch["uexp"] = pltpu.VMEM((rows, depth), BF16)
    if first:
        scratch["item_in"] = pltpu.VMEM(operands["item"].shape, F32)
    hbm = ("interactions", "item")
    operands = {
        name: in_hbm(x) if name in hbm else in_vmem(x) if name == "user_shape" else x
        for name, x in operands.items()}
    names = list(operands) + list(outs) + list(scratch)
    kernel = functools.partial(
        stratum_kernel, names, stratum=stratum, at=at, rows=rows, items=items,
        factor=factor, first=first, last=last, tail=tail, ahead=ahead)
    results = pl.pallas_call(
        kernel,
        out_shape=[jax.ShapeDtypeStruct(*spec) for spec in outs.values()],
        in_specs=[HBM_SPEC if name in hbm else VMEM_SPEC for name in operands],
        out_specs=[VMEM_SPEC] * len(outs),
        scratch_shapes=list(scratch.values()),
        compiler_params=PARAMS,
        cost_estimate=pl.CostEstimate(flops=1, bytes_accessed=1, transcendentals=0),
        name=f"stratum{stratum}_at{at}",
    )(*operands.values())
    return dict(zip(outs, results))


def user_log_kernel(*refs, at, rows, shp_at, factor, first, filled):
    acc, recv, shp_old, rte_in = refs[:4]
    rest = refs[5:] if filled else refs[4:]
    if first:
        out, rte_out, block, sem = rest
        beta = row_sum(acc[0:8, :] + recv[0:8, :])
        rte = 0.5 * rte_in[...] + 0.5 * (0.3 + factor * beta)
        rte_out[...] = rte
    else:
        out, block, sem = rest
        rte = rte_in[...]
    extra = 8 if first else 0

    def body(general):
        low = rte
        for t, step in tiles(rows):
            stat = acc[extra + t:extra + t + step, :] + recv[extra + t:extra + t + step, :]
            shp = 0.5 * shp_old[shp_at + t:shp_at + t + step, :] + 0.5 * (0.3 + factor * stat)
            block[t:t + step, :], part_low = log_tile(shp, rte, general)
            low = jnp.minimum(low, part_low)
        return low

    low = body(False)

    @pl.when(jnp.logical_not(above(low)))
    def _():
        body(True)

    copy = pltpu.make_async_copy(block, out.at[pl.ds(at, rows), :], sem)
    copy.start()
    copy.wait()


def user_log_call(at, rows, shp_at, total, depth, factor, first, operands, filled):
    out_shape = [jax.ShapeDtypeStruct((total, depth), BF16)]
    out_specs = [HBM_SPEC]
    if first:
        out_shape.append(jax.ShapeDtypeStruct((8, depth), F32))
        out_specs.append(VMEM_SPEC)
    operands = list(operands)
    in_specs = [VMEM_SPEC] * 4
    if filled is not None:
        operands.append(filled)
        in_specs.append(HBM_SPEC)
    return pl.pallas_call(
        functools.partial(user_log_kernel, at=at, rows=rows, shp_at=shp_at, factor=factor, first=first,
                          filled=filled is not None),
        out_shape=out_shape,
        in_specs=in_specs,
        out_specs=out_specs,
        input_output_aliases={} if filled is None else {4: 0},
        scratch_shapes=[pltpu.VMEM((rows, depth), BF16), pltpu.SemaphoreType.DMA],
        compiler_params=PARAMS,
        cost_estimate=pl.CostEstimate(
            flops=40 * rows * depth, bytes_accessed=rows * depth * 14, transcendentals=rows * depth),
        name=f"user_log_at{at}",
    )(*operands)


def item_log_kernel(item, _, out, *, items):
    rte = item[items:items + 8, :]

    def body(general):
        out[...], low = log_tile(item[0:items, :], rte, general)
        return low

    low = body(False)

    @pl.when(jnp.logical_not(above(jnp.minimum(low, rte))))
    def _():
        body(True)


def item_log_call(item, after, items, depth):
    return pl.pallas_call(
        functools.partial(item_log_kernel, items=items),
        out_shape=jax.ShapeDtypeStruct((items, depth), BF16),
        in_specs=[VMEM_SPEC, VMEM_SPEC],
        out_specs=VMEM_SPEC,
        compiler_params=PARAMS,
        cost_estimate=pl.CostEstimate(
            flops=40 * items * depth, bytes_accessed=items * depth * 6, transcendentals=items * depth),
        name="item_log",
    )(item, after)


def swapped(value, axis, mask):
    return lax.ppermute(value, axis, [(a, a ^ mask) for a in range(lax.axis_size(axis))])


def moved(choice, value, then=None, operands=()):
    def branch(mask, value, *operands):
        arrived = swapped(value, "users", mask)
        return arrived if then is None else then(arrived, *operands)

    choices = [functools.partial(branch, mask) for mask in range(1, lax.axis_size("users"))]
    return lax.switch(choice, choices, value, *operands)


def exchanged(value):
    size = lax.axis_size("items")
    if size == 1:
        return value, jnp.zeros_like(value)
    mask = 1
    while mask * 2 < size:
        value = value + swapped(value, "items", mask)
        mask *= 2
    return value, swapped(value, "items", mask)


def per_device(interactions, matchings, user_shape, item_shape):
    group = lax.axis_size("users")
    factor = float(group)
    users, depth = user_shape.shape
    items = item_shape.shape[0]
    sizes = chunk_rows(users)
    starts = [sum(sizes[:i]) for i in range(len(sizes))]
    count = len(sizes)

    item, choices = prepare_call(matchings, item_shape, group - 1)
    order = [(s, at, rows) for s in range(STRATA) for at, rows in zip(starts, sizes)]

    def opening(arrived, user_shape, interactions):
        return arrived, start_call(user_shape, interactions, sizes[0])

    item, (uexp, theta, counts) = moved(choices[0], item, opening, (user_shape, interactions))
    rte = None
    shp = [None] * count
    sums = [None] * count
    for stratum in range(STRATA):
        carried = {"theta": theta}
        for i, (at, rows) in enumerate(zip(starts, sizes)):
            first, last = i == 0, i == count - 1
            step = stratum * count + i
            ahead = order[step + 1] if step + 1 < len(order) else None
            tail = tail_rows(rows) if last and stratum == STRATA - 1 else 0
            operands = {"counts": counts}
            if ahead:
                operands["interactions"] = interactions
            if stratum == 0:
                operands["uexp_all"] = uexp
            else:
                operands["acc"], operands["recv"] = sums[i]
                if stratum == 1:
                    operands["user_shape"] = user_shape
                else:
                    operands["shp_old"] = shp[i]
                if not first:
                    operands["rte"] = rte
                elif stratum > 1:
                    operands["rte_old"] = rte
            if first:
                operands["item"] = item
            elif last:
                operands["item_kept"] = carried["item_kept"]
            if not first:
                operands["item_exp"] = carried["item_exp"]
                operands["istat"] = carried["istat"]
            if (stratum > 0 and not first) or (stratum == 0 and last):
                operands["theta"] = carried["theta"]
            out = stratum_call(
                stratum, at, rows, items, depth, factor, first, last, tail, ahead, operands)
            counts = out.get("counts_ahead")
            shp[i] = out.get("shp_new")
            sums[i] = exchanged(out["upart"])
            if tail:
                tail_sums = exchanged(out["upart_tail"])
            if first:
                rte = out.get("rte_new")
                carried["item_exp"] = out["item_exp_new"]
                carried["item_kept"] = out.get("item_kept")
            if last:
                item = out["item_new"]
            else:
                carried["istat"] = out["istat_new"]
                if stratum > 0:
                    carried["theta"] = out["theta_new"]
        if stratum + 1 < STRATA:
            item = moved(choices[stratum + 1], item)
        else:
            item = swapped(item, "users", group - 1)
    user_log = None
    pieces = [(at, rows, 0, sums[i], shp[i]) for i, (at, rows) in enumerate(zip(starts, sizes))]
    if tail:
        at, rows = starts[-1], sizes[-1] - tail
        pieces[-1:] = [(at, rows, 0, sums[-1], shp[-1]), (at + rows, tail, rows, tail_sums, shp[-1])]
    for i, (at, rows, shp_at, piece_sums, piece_shp) in enumerate(pieces):
        out = user_log_call(
            at, rows, shp_at, users, depth, factor, i == 0, (*piece_sums, piece_shp, rte), user_log)
        user_log = out[0]
        if i == 0:
            rte = out[1]
            item_log = item_log_call(item, rte, items, depth)
    return user_log, item_log


def solution(mesh):
    placed = (P(None, "users", "items"), P(), P("users", None), P(("users", "items"), None))
    return jax.shard_map(
        per_device,
        mesh=mesh,
        in_specs=placed,
        out_specs=(P("users", None), P(("users", "items"), None)),
        check_vma=False,
    )
```

profile of v0, /device:TPU:0, one launch (start us, length us, event | category | flops | bytes accessed | tf_op | source)
XLA Modules:
  0.0 60.8 jit_solution(102932813929915853)
XLA Ops:
  0.6 0.9 %prepare.1 = (f32[256,128]{1,0:T(8,128)S(1)}, s32[1]{0:T(128)S(4)}, s32[1]{0:T(128)S(4)}, s32[1]{0:T(128)S(4)}) custom-call(s32[3]{0:T(128)} %matchings_hbm.1, bf16[256,128]{1,0:T(8,128)(2,1)} %shape_hbm.1), custom_call_target="tpu_custom_call" | custom-call | tf_op jit(solution)/shard_map/prepare/pallas_call | solution.py:137
  1.5 7.4 %conditional.3 = (f32[256,128]{1,0:T(8,128)}, bf16[1280,128]{1,0:T(8,128)(2,1)S(1)}, f32[8,128]{1,0:T(8,128)S(1)}, bf16[640,256]{1,0:T(8,128)(2,1)S(1)}) conditional(s32[]{:T(128)} %bitcast, (f32[256,128]{1,0:T(8,128)S(1)}, bf16[1280,128]{1,0:T(8,128)(2,1)}, bf16[3,1280,256]{2,1,0:T(8,128)(2,1)}) %tuple.158, ...), branch_computations={%region_0.0_spmd, %region_1.0_spmd, %region_2.0_spmd, %region_3.0_... | conditional | flops 6553600 | bytes 1179720 | solution.py:445
  1.6 3.5 %collective-permute-start.6 = (f32[256,128]{1,0:T(8,128)S(1)}, f32[256,128]{1,0:T(8,128)}, u32[]{:S(2)}, u32[]{:S(2)}) collective-permute-start(f32[256,128]{1,0:T(8,128)S(1)} %get-tuple-element.188), channel_id=1, source_target_pairs={{0,14},{2,12},{4,10},{6,8},{8,6},{10,4},{12,2},{14,0},{16,30},{18,... | collective-permute-start | bytes 393224 | tf_op jit(solution)/shard_map/cond/branch_6_fun/ppermute | solution.py:436
  5.1 2.0 %user_start.21 = (bf16[1280,128]{1,0:T(8,128)(2,1)S(1)}, f32[8,128]{1,0:T(8,128)S(1)}, bf16[640,256]{1,0:T(8,128)(2,1)S(1)}) custom-call(bf16[1280,128]{1,0:T(8,128)(2,1)} %get-tuple-element.189.shape_hbm, bf16[3,1280,256]{2,1,0:T(8,128)(2,1)} %get-tuple-element.190.interactions), custom_call_target="tpu_custom_call" | custom-call | flops 6553600 | bytes 655360 | tf_op jit(solution)/shard_map/cond/branch_6_fun/user_start/pallas_call | solution.py:184
  7.0 1.9 %collective-permute-done.6 = f32[256,128]{1,0:T(8,128)} collective-permute-done((f32[256,128]{1,0:T(8,128)S(1)}, f32[256,128]{1,0:T(8,128)}, u32[]{:S(2)}, u32[]{:S(2)}) %collective-permute-start.6) | collective-permute-done | bytes 131104 | tf_op jit(solution)/shard_map/cond/branch_6_fun/ppermute | solution.py:436
  8.9 1.6 %stratum0_at0.1 = (f32[648,128]{1,0:T(8,128)S(1)}, bf16[256,128]{1,0:T(8,128)(2,1)S(1)}, f32[256,128]{1,0:T(8,128)S(1)}, f32[256,128]{1,0:T(8,128)S(1)}, bf16[640,256]{1,0:T(8,128)(2,1)S(1)}) custom-call(bf16[640,256]{1,0:T(8,128)(2,1)S(1)} %get-tuple-element.288.refs_0_, bf16[3,1280,256]{2,1,0:T(8,128)(2,1)} %refs_1_.9, ...), custom_call_target="tpu_custom_call" | custom-call | flops 1 | bytes 1 | tf_op jit(solution)/shard_map/stratum0_at0/pallas_call | solution.py:336
  10.5 0.0 copy-start
  10.6 2.3 %collective-permute-start.45 = (f32[648,128]{1,0:T(8,128)S(1)}, f32[648,128]{1,0:T(8,128)S(1)}, u32[]{:S(2)}, u32[]{:S(2)}) collective-permute-start(f32[648,128]{1,0:T(8,128)S(1)} %get-tuple-element.297.refs_2_), channel_id=1, source_target_pairs={{0,1},{1,0},{2,3},{3,2},{4,5},{5,4},{6,7},{7,6},{8,9},{9,8},{10,11... | collective-permute-start | bytes 995336 | tf_op jit(solution)/shard_map/ppermute | solution.py:436
  12.9 1.0 %stratum0_at640.1 = (f32[640,128]{1,0:T(8,128)S(1)}, f32[264,128]{1,0:T(8,128)S(1)}, bf16[640,256]{1,0:T(8,128)(2,1)S(1)}) custom-call(bf16[640,256]{1,0:T(8,128)(2,1)S(1)} %get-tuple-element.291.refs_0_, bf16[3,1280,256]{2,1,0:T(8,128)(2,1)} %refs_1_.9, bf16[1280,128]{1,0:T(8,128)(2,1)S(1)} %get-tuple-element.289.refs_2_, ...), custom_call_target="tpu_custom_call" | custom-call | flops 1 | bytes 1 | tf_op jit(solution)/shard_map/stratum0_at640/pallas_call | solution.py:336
  13.9 0.1 collective-permute-start.46
  14.0 1.5 %conditional.4 = (f32[264,128]{1,0:T(8,128)}) conditional(s32[]{:T(128)} %bitcast.1, f32[264,128]{1,0:T(8,128)S(1)} %get-tuple-element.299, f32[264,128]{1,0:T(8,128)S(1)} %get-tuple-element.299, f32[264,128]{1,0:T(8,128)S(1)} %get-tuple-element.299, f32[264,128]{1,0:T(8,128)S(1)} %get-tuple-element.299, ...), branch_computations={%region_15.0_spmd, %region_16.0_spmd, %region_17.0_spmd, %region_1... | conditional | bytes 540720 | solution.py:445
  14.0 0.1 collective-permute-start.15
  14.0 1.5 %collective-permute-done.15 = f32[264,128]{1,0:T(8,128)} collective-permute-done((f32[264,128]{1,0:T(8,128)S(1)}, f32[264,128]{1,0:T(8,128)}, u32[]{:S(2)}, u32[]{:S(2)}) %collective-permute-start.15) | collective-permute-done | bytes 135200 | tf_op jit(solution)/shard_map/cond/branch_0_fun/ppermute | solution.py:436
  15.5 5.9 %collective-permute-done.45.refs_3_ = f32[648,128]{1,0:T(8,128)S(1)} collective-permute-done((f32[648,128]{1,0:T(8,128)S(1)}, f32[648,128]{1,0:T(8,128)S(1)}, u32[]{:S(2)}, u32[]{:S(2)}) %collective-permute-start.45) | collective-permute-done | bytes 331808 | tf_op jit(solution)/shard_map/ppermute | solution.py:436
  21.4 0.0 copy-done
  21.5 1.8 %stratum1_at0.1 = (f32[648,128]{1,0:T(8,128)S(1)}, f32[640,128]{1,0:T(8,128)S(1)}, f32[8,128]{1,0:T(8,128)S(1)}, bf16[256,128]{1,0:T(8,128)(2,1)S(1)}, f32[264,1...) custom-call(bf16[640,256]{1,0:T(8,128)(2,1)S(1)} %get-tuple-element.296.refs_0_, ...), custom_call_target="tpu_custom_call" | custom-call | flops 1 | bytes 1 | tf_op jit(solution)/shard_map/stratum1_at0/pallas_call | solution.py:336
  23.2 2.1 %collective-permute-start.47 = (f32[648,128]{1,0:T(8,128)S(1)}, f32[648,128]{1,0:T(8,128)S(1)}, u32[]{:S(2)}, u32[]{:S(2)}) collective-permute-start(f32[648,128]{1,0:T(8,128)S(1)} %get-tuple-element.308.refs_2_), channel_id=1, source_target_pairs={{0,1},{1,0},{2,3},{3,2},{4,5},{5,4},{6,7},{7,6},{8,9},{9,8},{10,11... | collective-permute-start | bytes 995336 | tf_op jit(solution)/shard_map/ppermute | solution.py:436
  25.4 3.1 %collective-permute-done.46.refs_3_ = f32[640,128]{1,0:T(8,128)S(1)} collective-permute-done((f32[640,128]{1,0:T(8,128)S(1)}, f32[640,128]{1,0:T(8,128)S(1)}, u32[]{:S(2)}, u32[]{:S(2)}) %collective-permute-start.46) | collective-permute-done | bytes 327712 | tf_op jit(solution)/shard_map/ppermute | solution.py:436
  28.5 1.0 %stratum1_at640.1 = (f32[640,128]{1,0:T(8,128)S(1)}, f32[640,128]{1,0:T(8,128)S(1)}, f32[264,128]{1,0:T(8,128)S(1)}, bf16[640,256]{1,0:T(8,128)(2,1)S(1)}) custom-call(bf16[640,256]{1,0:T(8,128)(2,1)S(1)} %get-tuple-element.300.refs_0_, bf16[3,1280,256]{2,1,0:T(8,128)(2,1)} %refs_1_.9, f32[640,128]{1,0:T(8,128)S(1)} %get-tuple-element.301.refs_2_, ...), custom_call_target="tpu_custom_call" | custom-call | flops 1 | bytes 1 | tf_op jit(solution)/shard_map/stratum1_at640/pallas_call | solution.py:336
  29.5 2.1 %collective-permute-start.48 = (f32[640,128]{1,0:T(8,128)S(1)}, f32[640,128]{1,0:T(8,128)S(1)}, u32[]{:S(2)}, u32[]{:S(2)}) collective-permute-start(f32[640,128]{1,0:T(8,128)S(1)} %get-tuple-element.313.refs_1_), channel_id=1, source_target_pairs={{0,1},{1,0},{2,3},{3,2},{4,5},{5,4},{6,7},{7,6},{8,9},{9,8},{10,11... | collective-permute-start | bytes 983048 | tf_op jit(solution)/shard_map/ppermute | solution.py:436
  31.6 9.5 %conditional.5 = (f32[264,128]{1,0:T(8,128)}) conditional(s32[]{:T(128)} %bitcast.2, f32[264,128]{1,0:T(8,128)S(1)} %get-tuple-element.311, f32[264,128]{1,0:T(8,128)S(1)} %get-tuple-element.311, f32[264,128]{1,0:T(8,128)S(1)} %get-tuple-element.311, f32[264,128]{1,0:T(8,128)S(1)} %get-tuple-element.311, ...), branch_computations={%region_30.0_spmd, %region_31.0_spmd, %region_32.0_spmd, %region_3... | conditional | bytes 540720 | solution.py:445
  31.6 0.4 collective-permute-start.38
  32.0 9.2 %collective-permute-done.38 = f32[264,128]{1,0:T(8,128)} collective-permute-done((f32[264,128]{1,0:T(8,128)S(1)}, f32[264,128]{1,0:T(8,128)}, u32[]{:S(2)}, u32[]{:S(2)}) %collective-permute-start.38) | collective-permute-done | bytes 135200 | tf_op jit(solution)/shard_map/cond/branch_8_fun/ppermute | solution.py:436
  41.1 0.0 collective-permute-done.47.refs_3_
  41.1 1.6 %stratum2_at0.1 = (f32[648,128]{1,0:T(8,128)S(1)}, f32[640,128]{1,0:T(8,128)S(1)}, f32[8,128]{1,0:T(8,128)S(1)}, bf16[256,128]{1,0:T(8,128)(2,1)S(1)}, f32[264,1...) custom-call(bf16[640,256]{1,0:T(8,128)(2,1)S(1)} %get-tuple-element.307.refs_0_, ...), custom_call_target="tpu_custom_call" | custom-call | flops 1 | bytes 1 | tf_op jit(solution)/shard_map/stratum2_at0/pallas_call | solution.py:336
  42.8 0.1 collective-permute-start.50
  42.8 0.0 collective-permute-done.48.refs_2_
  42.8 0.9 %stratum2_at640.1 = (f32[320,128]{1,0:T(8,128)S(1)}, f32[320,128]{1,0:T(8,128)S(1)}, f32[640,128]{1,0:T(8,128)S(1)}, f32[264,128]{1,0:T(8,128)S(1)}) custom-call(bf16[640,256]{1,0:T(8,128)(2,1)S(1)} %get-tuple-element.312.refs_0_, f32[640,128]{1,0:T(8,128)S(1)} %get-tuple-element.313.refs_1_, f32[640,128]{1,0:T(8,128)S(1)} %collective-permute-done.48.refs_2_, ...), custom_call_target="tpu_custom_call" | custom-call | flops 1 | bytes 1 | tf_op jit(solution)/shard_map/stratum2_at640/pallas_call | solution.py:336
  43.8 2.1 %collective-permute-start.51 = (f32[320,128]{1,0:T(8,128)S(1)}, f32[320,128]{1,0:T(8,128)S(1)}, u32[]{:S(2)}, u32[]{:S(2)}) collective-permute-start(f32[320,128]{1,0:T(8,128)S(1)} %get-tuple-element.325.refs_0_), channel_id=1, source_target_pairs={{0,1},{1,0},{2,3},{3,2},{4,5},{5,4},{6,7},{7,6},{8,9},{9,8},{10,11... | collective-permute-start | bytes 491528 | tf_op jit(solution)/shard_map/ppermute | solution.py:436
  45.8 0.1 collective-permute-start.49
  45.9 2.5 %collective-permute-start.52 = (f32[264,128]{1,0:T(8,128)S(1)}, f32[264,128]{1,0:T(8,128)S(1)}, u32[]{:S(2)}, u32[]{:S(2)}) collective-permute-start(f32[264,128]{1,0:T(8,128)S(1)} %get-tuple-element.327), channel_id=1, source_target_pairs={{0,30},{2,28},{4,26},{6,24},{8,22},{10,20},{12,18},{14,16},{16,14}... | collective-permute-start | bytes 405512 | tf_op jit(solution)/shard_map/ppermute | solution.py:436
  48.4 5.0 %collective-permute-done.50.refs_1_ = f32[648,128]{1,0:T(8,128)S(1)} collective-permute-done((f32[648,128]{1,0:T(8,128)S(1)}, f32[648,128]{1,0:T(8,128)S(1)}, u32[]{:S(2)}, u32[]{:S(2)}) %collective-permute-start.50) | collective-permute-done | bytes 331808 | tf_op jit(solution)/shard_map/ppermute | solution.py:436
  53.5 1.3 %user_log_at0.1 = (bf16[1280,128]{1,0:T(8,128)(2,1)}, f32[8,128]{1,0:T(8,128)S(1)}) custom-call(f32[648,128]{1,0:T(8,128)S(1)} %get-tuple-element.322.refs_0_, f32[648,128]{1,0:T(8,128)S(1)} %collective-permute-done.50.refs_1_, f32[640,128]{1,0:T(8,128)S(1)} %get-tuple-element.323.refs_2_, f32[8,128]{1,0:T(8,128)S(1)} %get-tuple-element.315.refs_4_.refs_3_), custom_call_target="tpu_custom_call" | custom-call | flops 3276800 | bytes 1146880 | tf_op jit(solution)/shard_map/user_log_at0/pallas_call | solution.py:393
  54.7 0.0 collective-permute-done.52.item
  54.7 0.9 %item_log.1 = bf16[256,128]{1,0:T(8,128)(2,1)} custom-call(f32[264,128]{1,0:T(8,128)S(1)} %collective-permute-done.52.item, f32[8,128]{1,0:T(8,128)S(1)} %get-tuple-element.324.refs_3_._), custom_call_target="tpu_custom_call" | custom-call | flops 1310720 | bytes 196608 | tf_op jit(solution)/shard_map/item_log/pallas_call | solution.py:423
  55.7 1.3 %collective-permute-done.51.refs_1_ = f32[320,128]{1,0:T(8,128)S(1)} collective-permute-done((f32[320,128]{1,0:T(8,128)S(1)}, f32[320,128]{1,0:T(8,128)S(1)}, u32[]{:S(2)}, u32[]{:S(2)}) %collective-permute-start.51) | collective-permute-done | bytes 163872 | tf_op jit(solution)/shard_map/ppermute | solution.py:436
  57.0 1.0 %user_log_at640.1.refs_4_ = bf16[1280,128]{1,0:T(8,128)(2,1)} custom-call(f32[320,128]{1,0:T(8,128)S(1)} %get-tuple-element.325.refs_0_, f32[320,128]{1,0:T(8,128)S(1)} %collective-permute-done.51.refs_1_, f32[640,128]{1,0:T(8,128)S(1)} %get-tuple-element.321.refs_2_, f32[8,128]{1,0:T(8,128)S(1)} %get-tuple-element.324.refs_3_._, ...), custom_call_target="tpu_custom_call", output_to_operand_aliasing={{}: (4, {})} | custom-call | flops 1638400 | bytes 573440 | tf_op jit(solution)/shard_map/user_log_at640/pallas_call | solution.py:393
  58.0 1.7 %collective-permute-done.49.refs_1_ = f32[320,128]{1,0:T(8,128)S(1)} collective-permute-done((f32[320,128]{1,0:T(8,128)S(1)}, f32[320,128]{1,0:T(8,128)S(1)}, u32[]{:S(2)}, u32[]{:S(2)}) %collective-permute-start.49) | collective-permute-done | bytes 163872 | tf_op jit(solution)/shard_map/ppermute | solution.py:436
  59.7 1.0 %user_log_at960.1 = bf16[1280,128]{1,0:T(8,128)(2,1)} custom-call(f32[320,128]{1,0:T(8,128)S(1)} %get-tuple-element.320.refs_0_, f32[320,128]{1,0:T(8,128)S(1)} %collective-permute-done.49.refs_1_, f32[640,128]{1,0:T(8,128)S(1)} %get-tuple-element.321.refs_2_, f32[8,128]{1,0:T(8,128)S(1)} %get-tuple-element.324.refs_3_._, ...), custom_call_target="tpu_custom_call", output_to_operand_aliasing={{}: (4, {})} | custom-call | flops 1638400 | bytes 573440 | tf_op jit(solution)/shard_map/user_log_at960/pallas_call | solution.py:393
Async XLA Ops:
  1.6 7.4 %collective-permute-start.6 = (f32[256,128]{1,0:T(8,128)S(1)}, f32[256,128]{1,0:T(8,128)}, u32[]{:S(2)}, u32[]{:S(2)}) collective-permute-start(f32[256,128]{1,0:T(8,128)S(1)} %get-tuple-element.188), channel_id=1, source_target_pairs={{0,14},{2,12},{4,10},{6,8},{8,6},{10,4},{12,2},{14,0},{16,30},{18,... | collective-permute-start | bytes 393224 | tf_op jit(solution)/shard_map/cond/branch_6_fun/ppermute | solution.py:436
  10.5 10.9 %copy-start = (bf16[1280,128]{1,0:T(8,128)(2,1)S(1)}, bf16[1280,128]{1,0:T(8,128)(2,1)}, u32[]{:S(2)}) copy-start(bf16[1280,128]{1,0:T(8,128)(2,1)} %refs_4_.3) | copy-start | bytes 983044
  10.6 10.9 %collective-permute-start.45 = (f32[648,128]{1,0:T(8,128)S(1)}, f32[648,128]{1,0:T(8,128)S(1)}, u32[]{:S(2)}, u32[]{:S(2)}) collective-permute-start(f32[648,128]{1,0:T(8,128)S(1)} %get-tuple-element.297.refs_2_), channel_id=1, source_target_pairs={{0,1},{1,0},{2,3},{3,2},{4,5},{5,4},{6,7},{7,6},{8,9},{9,8},{10,11... | collective-permute-start | bytes 995336 | tf_op jit(solution)/shard_map/ppermute | solution.py:436
  13.9 14.6 %collective-permute-start.46 = (f32[640,128]{1,0:T(8,128)S(1)}, f32[640,128]{1,0:T(8,128)S(1)}, u32[]{:S(2)}, u32[]{:S(2)}) collective-permute-start(f32[640,128]{1,0:T(8,128)S(1)} %get-tuple-element.301.refs_2_), channel_id=1, source_target_pairs={{0,1},{1,0},{2,3},{3,2},{4,5},{5,4},{6,7},{7,6},{8,9},{9,8},{10,11... | collective-permute-start | bytes 983048 | tf_op jit(solution)/shard_map/ppermute | solution.py:436
  14.0 1.5 %collective-permute-start.15 = (f32[264,128]{1,0:T(8,128)S(1)}, f32[264,128]{1,0:T(8,128)}, u32[]{:S(2)}, u32[]{:S(2)}) collective-permute-start(f32[264,128]{1,0:T(8,128)S(1)} %param.15), channel_id=1, source_target_pairs={{0,2},{2,0},{4,6},{6,4},{8,10},{10,8},{12,14},{14,12},{16,18},{18,... | collective-permute-start | bytes 405512 | tf_op jit(solution)/shard_map/cond/branch_0_fun/ppermute | solution.py:436
  23.2 17.9 %collective-permute-start.47 = (f32[648,128]{1,0:T(8,128)S(1)}, f32[648,128]{1,0:T(8,128)S(1)}, u32[]{:S(2)}, u32[]{:S(2)}) collective-permute-start(f32[648,128]{1,0:T(8,128)S(1)} %get-tuple-element.308.refs_2_), channel_id=1, source_target_pairs={{0,1},{1,0},{2,3},{3,2},{4,5},{5,4},{6,7},{7,6},{8,9},{9,8},{10,11... | collective-permute-start | bytes 995336 | tf_op jit(solution)/shard_map/ppermute | solution.py:436
  29.5 13.4 %collective-permute-start.48 = (f32[640,128]{1,0:T(8,128)S(1)}, f32[640,128]{1,0:T(8,128)S(1)}, u32[]{:S(2)}, u32[]{:S(2)}) collective-permute-start(f32[640,128]{1,0:T(8,128)S(1)} %get-tuple-element.313.refs_1_), channel_id=1, source_target_pairs={{0,1},{1,0},{2,3},{3,2},{4,5},{5,4},{6,7},{7,6},{8,9},{9,8},{10,11... | collective-permute-start | bytes 983048 | tf_op jit(solution)/shard_map/ppermute | solution.py:436
  31.6 9.5 %collective-permute-start.38 = (f32[264,128]{1,0:T(8,128)S(1)}, f32[264,128]{1,0:T(8,128)}, u32[]{:S(2)}, u32[]{:S(2)}) collective-permute-start(f32[264,128]{1,0:T(8,128)S(1)} %param.38), channel_id=1, source_target_pairs={{0,18},{2,16},{4,22},{6,20},{8,26},{10,24},{12,30},{14,28},{16,2},... | collective-permute-start | bytes 405512 | tf_op jit(solution)/shard_map/cond/branch_8_fun/ppermute | solution.py:436
  42.8 10.7 %collective-permute-start.50 = (f32[648,128]{1,0:T(8,128)S(1)}, f32[648,128]{1,0:T(8,128)S(1)}, u32[]{:S(2)}, u32[]{:S(2)}) collective-permute-start(f32[648,128]{1,0:T(8,128)S(1)} %get-tuple-element.322.refs_0_), channel_id=1, source_target_pairs={{0,1},{1,0},{2,3},{3,2},{4,5},{5,4},{6,7},{7,6},{8,9},{9,8},{10,11... | collective-permute-start | bytes 995336 | tf_op jit(solution)/shard_map/ppermute | solution.py:436
  43.8 13.2 %collective-permute-start.51 = (f32[320,128]{1,0:T(8,128)S(1)}, f32[320,128]{1,0:T(8,128)S(1)}, u32[]{:S(2)}, u32[]{:S(2)}) collective-permute-start(f32[320,128]{1,0:T(8,128)S(1)} %get-tuple-element.325.refs_0_), channel_id=1, source_target_pairs={{0,1},{1,0},{2,3},{3,2},{4,5},{5,4},{6,7},{7,6},{8,9},{9,8},{10,11... | collective-permute-start | bytes 491528 | tf_op jit(solution)/shard_map/ppermute | solution.py:436
  45.8 13.8 %collective-permute-start.49 = (f32[320,128]{1,0:T(8,128)S(1)}, f32[320,128]{1,0:T(8,128)S(1)}, u32[]{:S(2)}, u32[]{:S(2)}) collective-permute-start(f32[320,128]{1,0:T(8,128)S(1)} %get-tuple-element.320.refs_0_), channel_id=1, source_target_pairs={{0,1},{1,0},{2,3},{3,2},{4,5},{5,4},{6,7},{7,6},{8,9},{9,8},{10,11... | collective-permute-start | bytes 491528 | tf_op jit(solution)/shard_map/ppermute | solution.py:436
  45.9 8.8 %collective-permute-start.52 = (f32[264,128]{1,0:T(8,128)S(1)}, f32[264,128]{1,0:T(8,128)S(1)}, u32[]{:S(2)}, u32[]{:S(2)}) collective-permute-start(f32[264,128]{1,0:T(8,128)S(1)} %get-tuple-element.327), channel_id=1, source_target_pairs={{0,30},{2,28},{4,26},{6,24},{8,22},{10,20},{12,18},{14,16},{16,14}... | collective-permute-start | bytes 405512 | tf_op jit(solution)/shard_map/ppermute | solution.py:436
where the time goes:
time: 61.9 us; the launch traced here: 60.8 us
  waiting for transfers between devices  29.7 us (48%)
  starting transfers between devices  15.3 us (25%)
  Pallas kernels  14.9 us (24%)
  between operations  0.91 us (1%)
    ppermute x11, waiting for transfers between devices, swapped(): lax.ppermute(value, axis, [(a, a ^ mask) for a in range(lax.axis_size(axi...  29.7 us
    ppermute x11, starting transfers between devices, swapped(): lax.ppermute(value, axis, [(a, a ^ mask) for a in range(lax.axis_size(axi...  15.3 us
    pallas_call x6, Pallas kernels, stratum_call(): pl.pallas_call(kernel, out_shape=[jax.ShapeDtypeStruct(*spec) for spec in...  7.89 us
    pallas_call x3, Pallas kernels, user_log_call(): pl.pallas_call(functools.partial(user_log_kernel, at=at, rows=rows, shp_a...  3.23 us
    pallas_call x1, Pallas kernels, start_call(): pl.pallas_call(start_kernel, out_shape=[pltpu.VMEM((rows, depth), BF16),...  1.95 us
  transfers between devices with their start and end apart: 11, of which 8 were waited for; matrix products, arithmetic and copies ran while one was open for 0% of the time, Pallas kernels for 19%

commit v1 on v0

--- a/solution.py
+++ b/solution.py
@@ -195,7 +195,11 @@
     )(in_hbm(user_shape), in_hbm(interactions))
 
 
-def stratum_kernel(names, *refs, stratum, at, rows, items, factor, first, last, tail, ahead):
+def item_sums(ratios, uexp):
+    return lax.dot_general(ratios[...], uexp[...], (((0,), (0,)), ((), ())), preferred_element_type=F32)
+
+
+def stratum_kernel(names, *refs, stratum, at, rows, items, factor, first, last, earlier, tail, ahead):
     ref = dict(zip(names, refs))
     copies = {}
 
@@ -203,12 +207,14 @@
         copies[name] = pltpu.make_async_copy(source, target, ref["sems"].at[len(copies)])
         copies[name].start()
 
-    if "item_in" in ref:
-        fetch("item", ref["item"], ref["item_in"])
+    if first:
+        fetch("item", ref["item"], ref["item_kept"])
     if ahead:
         fetch("ahead", ref["interactions"].at[ahead[0], pl.ds(ahead[1], ahead[2]), :], ref["counts_ahead"])
     upart, counts, ratios, denominator = ref["upart"], ref["counts"], ref["ratios"], ref["denominator"]
-    uexp = ref["uexp_all"].at[pl.ds(at, rows), :] if stratum == 0 else ref["uexp"]
+    uexp = ref["uexp"]
+    if stratum == 0:
+        uexp[...] = ref["uexp_all"][at:at + rows, :]
     extra = 8 if first else 0
 
     def wait(name, general):
@@ -243,12 +249,8 @@
 
         if first:
             wait("item", general)
-            item = ref["item_in"] if "item_in" in ref else ref["item"]
-            if not last:
-                ref["item_kept"][...] = item[...]
-        elif last:
+        if first or last:
             item = ref["item_kept"]
-        if first or last:
             item_rte = None if stratum == 0 else item[items:items + 8, :]
         if first:
             value, sums, low = exp_tile(item[0:items, :], item_rte, general)
@@ -271,18 +273,16 @@
         upart[extra:extra + rows - tail, :] = user_sums[0:rows - tail, :]
         if tail:
             ref["upart_tail"][...] = user_sums[rows - tail:, :]
-        istat = lax.dot_general(ratios[...], uexp[...], (((0,), (0,)), ((), ())), preferred_element_type=F32)
-        if not first:
-            istat = istat + ref["istat"][...]
         if last:
+            istat = item_sums(ratios, uexp)
+            for i in range(earlier):
+                istat = istat + item_sums(ref[f"ratios{i}"], ref[f"uexp{i}"])
             old = 1.0 if item_rte is None else item_rte
             ref["item_new"][0:items, :] = 0.5 * item[0:items, :] + 0.5 * (
                 0.3 + factor * (item_exp.astype(F32) * istat))
             ref["item_new"][items:items + 8, :] = 0.5 * old + 0.5 * (0.3 + factor * row_sum(theta))
-        else:
-            ref["istat_new"][...] = istat
-            if stratum > 0:
-                ref["theta_new"][...] = theta
+        elif stratum > 0:
+            ref["theta_new"][...] = theta
         return functools.reduce(jnp.minimum, lows) if lows else None
 
     low = body(False)
@@ -295,7 +295,7 @@
     wait("ahead", False)
 
 
-def stratum_call(stratum, at, rows, items, depth, factor, first, last, tail, ahead, operands):
+def stratum_call(stratum, at, rows, items, depth, factor, first, last, earlier, tail, ahead, operands):
     extra = 8 if first else 0
     outs = {"upart": ((rows + extra - tail, depth), F32)}
     if tail:
@@ -306,25 +306,24 @@
         outs["rte_new"] = ((8, depth), F32)
     if first:
         outs["item_exp_new"] = ((items, depth), BF16)
-    if first and not last:
+    if first:
         outs["item_kept"] = (operands["item"].shape, F32)
     if last:
         outs["item_new"] = ((items + 8, depth), F32)
     else:
-        outs["istat_new"] = ((items, depth), F32)
+        outs["ratios"] = ((rows, items), BF16)
+        outs["uexp"] = ((rows, depth), BF16)
         if stratum > 0:
             outs["theta_new"] = ((8, depth), F32)
     if ahead:
         outs["counts_ahead"] = ((ahead[2], items), BF16)
     scratch = {
-        "ratios": pltpu.VMEM((rows, items), BF16),
         "denominator": pltpu.VMEM((rows, items), F32),
         "sems": pltpu.SemaphoreType.DMA((2,)),
     }
-    if stratum > 0:
+    if last:
+        scratch["ratios"] = pltpu.VMEM((rows, items), BF16)
         scratch["uexp"] = pltpu.VMEM((rows, depth), BF16)
-    if first:
-        scratch["item_in"] = pltpu.VMEM(operands["item"].shape, F32)
     hbm = ("interactions", "item")
     operands = {
         name: in_hbm(x) if name in hbm else in_vmem(x) if name == "user_shape" else x
@@ -332,7 +331,7 @@
     names = list(operands) + list(outs) + list(scratch)
     kernel = functools.partial(
         stratum_kernel, names, stratum=stratum, at=at, rows=rows, items=items,
-        factor=factor, first=first, last=last, tail=tail, ahead=ahead)
+        factor=factor, first=first, last=last, earlier=earlier, tail=tail, ahead=ahead)
     results = pl.pallas_call(
         kernel,
         out_shape=[jax.ShapeDtypeStruct(*spec) for spec in outs.values()],
@@ -349,14 +348,12 @@
 def user_log_kernel(*refs, at, rows, shp_at, factor, first, filled):
     acc, recv, shp_old, rte_in = refs[:4]
     rest = refs[5:] if filled else refs[4:]
+    out, *rte_out, block, sem = rest
+    rte = rte_in[...]
     if first:
-        out, rte_out, block, sem = rest
-        beta = row_sum(acc[0:8, :] + recv[0:8, :])
-        rte = 0.5 * rte_in[...] + 0.5 * (0.3 + factor * beta)
-        rte_out[...] = rte
-    else:
-        out, block, sem = rest
-        rte = rte_in[...]
+        rte = 0.5 * rte + 0.5 * (0.3 + factor * row_sum(acc[0:8, :] + recv[0:8, :]))
+    for ref in rte_out:
+        ref[...] = rte
     extra = 8 if first else 0
 
     def body(general):
@@ -382,7 +379,7 @@
 def user_log_call(at, rows, shp_at, total, depth, factor, first, operands, filled):
     out_shape = [jax.ShapeDtypeStruct((total, depth), BF16)]
     out_specs = [HBM_SPEC]
-    if first:
+    if at + rows < total:
         out_shape.append(jax.ShapeDtypeStruct((8, depth), F32))
         out_specs.append(VMEM_SPEC)
     operands = list(operands)
@@ -477,6 +474,7 @@
     sums = [None] * count
     for stratum in range(STRATA):
         carried = {"theta": theta}
+        earlier = {}
         for i, (at, rows) in enumerate(zip(starts, sizes)):
             first, last = i == 0, i == count - 1
             step = stratum * count + i
@@ -503,11 +501,12 @@
                 operands["item_kept"] = carried["item_kept"]
             if not first:
                 operands["item_exp"] = carried["item_exp"]
-                operands["istat"] = carried["istat"]
+            if last:
+                operands.update(earlier)
             if (stratum > 0 and not first) or (stratum == 0 and last):
                 operands["theta"] = carried["theta"]
             out = stratum_call(
-                stratum, at, rows, items, depth, factor, first, last, tail, ahead, operands)
+                stratum, at, rows, items, depth, factor, first, last, i, tail, ahead, operands)
             counts = out.get("counts_ahead")
             shp[i] = out.get("shp_new")
             sums[i] = exchanged(out["upart"])
@@ -516,11 +515,11 @@
             if first:
                 rte = out.get("rte_new")
                 carried["item_exp"] = out["item_exp_new"]
-                carried["item_kept"] = out.get("item_kept")
+                carried["item_kept"] = out["item_kept"]
             if last:
                 item = out["item_new"]
             else:
-                carried["istat"] = out["istat_new"]
+                earlier[f"ratios{i}"], earlier[f"uexp{i}"] = out["ratios"], out["uexp"]
                 if stratum > 0:
                     carried["theta"] = out["theta_new"]
         if stratum + 1 < STRATA:
@@ -533,11 +532,10 @@
         at, rows = starts[-1], sizes[-1] - tail
         pieces[-1:] = [(at, rows, 0, sums[-1], shp[-1]), (at + rows, tail, rows, tail_sums, shp[-1])]
     for i, (at, rows, shp_at, piece_sums, piece_shp) in enumerate(pieces):
-        out = user_log_call(
+        user_log, *rest = user_log_call(
             at, rows, shp_at, users, depth, factor, i == 0, (*piece_sums, piece_shp, rte), user_log)
-        user_log = out[0]
-        if i == 0:
-            rte = out[1]
+        rte = rest[0] if rest else rte
+        if i == max(len(pieces) - 2, 0):
             item_log = item_log_call(item, rte, items, depth)
     return user_log, item_log
 

time: 61.9 us -> 56.2 us (0.908); the launches traced: 60.8 us -> 56.4 us
  waiting for transfers between devices: 29.7 us -> 23.3 us
  starting transfers between devices: 15.3 us -> 17.5 us
    ppermute x11, waiting for transfers between devices: 29.7 us -> 23.3 us  [swapped(): lax.ppermute(value, axis, [(a, a ^ mask) for a in range(lax.axis_size(axi...]
    ppermute x11, starting transfers between devices: 15.3 us -> 17.5 us  [swapped(): lax.ppermute(value, axis, [(a, a ^ mask) for a in range(lax.axis_size(axi...]
  transfers between devices with their start and end apart: 11 -> 11, of which waited for: 8 -> 8; matrix products, arithmetic and copies ran while one was open for 0% -> 0% of each run, Pallas kernels for 19% -> 20%
where the time goes in v1:
time: 56.2 us; the launch traced here: 56.4 us
  waiting for transfers between devices  23.3 us (41%)
  starting transfers between devices  17.5 us (31%)
  Pallas kernels  14.7 us (26%)
  between operations  0.89 us (2%)
    ppermute x11, waiting for transfers between devices, swapped(): lax.ppermute(value, axis, [(a, a ^ mask) for a in range(lax.axis_size(axi...  23.3 us
    ppermute x11, starting transfers between devices, swapped(): lax.ppermute(value, axis, [(a, a ^ mask) for a in range(lax.axis_size(axi...  17.5 us
    pallas_call x6, Pallas kernels, stratum_call(): pl.pallas_call(kernel, out_shape=[jax.ShapeDtypeStruct(*spec) for spec in...  7.68 us
    pallas_call x3, Pallas kernels, user_log_call(): pl.pallas_call(functools.partial(user_log_kernel, at=at, rows=rows, shp_a...  3.23 us
    pallas_call x1, Pallas kernels, start_call(): pl.pallas_call(start_kernel, out_shape=[pltpu.VMEM((rows, depth), BF16),...  1.95 us
  transfers between devices with their start and end apart: 11, of which 8 were waited for; matrix products, arithmetic and copies ran while one was open for 0% of the time, Pallas kernels for 20%

profile of v1, /device:TPU:0, one launch (start us, length us, event | category | flops | bytes accessed | tf_op | source)
XLA Modules:
  0.0 56.4 jit_solution(3425069093725725473)
XLA Ops:
  0.6 0.9 %prepare.1 = (f32[256,128]{1,0:T(8,128)S(1)}, s32[1]{0:T(128)S(4)}, s32[1]{0:T(128)S(4)}, s32[1]{0:T(128)S(4)}) custom-call(s32[3]{0:T(128)} %matchings_hbm.1, bf16[256,128]{1,0:T(8,128)(2,1)} %shape_hbm.1), custom_call_target="tpu_custom_call" | custom-call | tf_op jit(solution)/shard_map/prepare/pallas_call | solution.py:137
  1.5 7.7 %conditional.3 = (f32[256,128]{1,0:T(8,128)}, bf16[1280,128]{1,0:T(8,128)(2,1)S(1)}, f32[8,128]{1,0:T(8,128)S(1)}, bf16[640,256]{1,0:T(8,128)(2,1)S(1)}) conditional(s32[]{:T(128)} %bitcast, (f32[256,128]{1,0:T(8,128)S(1)}, bf16[1280,128]{1,0:T(8,128)(2,1)}, bf16[3,1280,256]{2,1,0:T(8,128)(2,1)}) %tuple.158, ...), branch_computations={%region_0.0_spmd, %region_1.0_spmd, %region_2.0_spmd, %region_3.0_... | conditional | flops 6553600 | bytes 1179720 | solution.py:442
  1.6 4.0 %collective-permute-start.5 = (f32[256,128]{1,0:T(8,128)S(1)}, f32[256,128]{1,0:T(8,128)}, u32[]{:S(2)}, u32[]{:S(2)}) collective-permute-start(f32[256,128]{1,0:T(8,128)S(1)} %get-tuple-element.182), channel_id=1, source_target_pairs={{0,12},{2,14},{4,8},{6,10},{8,4},{10,6},{12,0},{14,2},{16,28},{18,... | collective-permute-start | bytes 393224 | tf_op jit(solution)/shard_map/cond/branch_5_fun/ppermute | solution.py:433
  5.6 2.0 %user_start.20 = (bf16[1280,128]{1,0:T(8,128)(2,1)S(1)}, f32[8,128]{1,0:T(8,128)S(1)}, bf16[640,256]{1,0:T(8,128)(2,1)S(1)}) custom-call(bf16[1280,128]{1,0:T(8,128)(2,1)} %get-tuple-element.183.shape_hbm, bf16[3,1280,256]{2,1,0:T(8,128)(2,1)} %get-tuple-element.184.interactions), custom_call_target="tpu_custom_call" | custom-call | flops 6553600 | bytes 655360 | tf_op jit(solution)/shard_map/cond/branch_5_fun/user_start/pallas_call | solution.py:184
  7.6 1.6 %collective-permute-done.5 = f32[256,128]{1,0:T(8,128)} collective-permute-done((f32[256,128]{1,0:T(8,128)S(1)}, f32[256,128]{1,0:T(8,128)}, u32[]{:S(2)}, u32[]{:S(2)}) %collective-permute-start.5) | collective-permute-done | bytes 131104 | tf_op jit(solution)/shard_map/cond/branch_5_fun/ppermute | solution.py:433
  9.2 1.5 %stratum0_at0.1 = (f32[648,128]{1,0:T(8,128)S(1)}, bf16[256,128]{1,0:T(8,128)(2,1)S(1)}, f32[256,128]{1,0:T(8,128)S(1)}, bf16[640,256]{1,0:T(8,128)(2,1)S(1)}, b...) custom-call(bf16[640,256]{1,0:T(8,128)(2,1)S(1)} %get-tuple-element.293.refs_0_, bf16[3,1280,256]{2,1,0:T(8,128)(2,1)} %refs_1_.9, ...), custom_call_target="tpu_custom_call" | custom-call | flops 1 | bytes 1 | tf_op jit(solution)/shard_map/stratum0_at0/pallas_call | solution.py:335
  10.7 0.0 copy-start
  10.7 1.7 %collective-permute-start.45 = (f32[648,128]{1,0:T(8,128)S(1)}, f32[648,128]{1,0:T(8,128)S(1)}, u32[]{:S(2)}, u32[]{:S(2)}) collective-permute-start(f32[648,128]{1,0:T(8,128)S(1)} %get-tuple-element.303.refs_2_), channel_id=1, source_target_pairs={{0,1},{1,0},{2,3},{3,2},{4,5},{5,4},{6,7},{7,6},{8,9},{9,8},{10,11... | collective-permute-start | bytes 995336 | tf_op jit(solution)/shard_map/ppermute | solution.py:433
  12.4 1.0 %stratum0_at640.1 = (f32[640,128]{1,0:T(8,128)S(1)}, f32[264,128]{1,0:T(8,128)S(1)}, bf16[640,256]{1,0:T(8,128)(2,1)S(1)}) custom-call(bf16[640,256]{1,0:T(8,128)(2,1)S(1)} %get-tuple-element.296.refs_0_, bf16[3,1280,256]{2,1,0:T(8,128)(2,1)} %refs_1_.9, bf16[1280,128]{1,0:T(8,128)(2,1)S(1)} %get-tuple-element.294.refs_2_, ...), custom_call_target="tpu_custom_call" | custom-call | flops 1 | bytes 1 | tf_op jit(solution)/shard_map/stratum0_at640/pallas_call | solution.py:335
  13.4 0.5 collective-permute-start.46
  13.9 6.6 %conditional.4 = (f32[264,128]{1,0:T(8,128)}) conditional(s32[]{:T(128)} %bitcast.1, f32[264,128]{1,0:T(8,128)S(1)} %get-tuple-element.305, f32[264,128]{1,0:T(8,128)S(1)} %get-tuple-element.305, f32[264,128]{1,0:T(8,128)S(1)} %get-tuple-element.305, f32[264,128]{1,0:T(8,128)S(1)} %get-tuple-element.305, ...), branch_computations={%region_15.0_spmd, %region_16.0_spmd, %region_17.0_spmd, %region_1... | conditional | bytes 540720 | solution.py:442
  13.9 0.6 %collective-permute-start.21 = (f32[264,128]{1,0:T(8,128)S(1)}, f32[264,128]{1,0:T(8,128)}, u32[]{:S(2)}, u32[]{:S(2)}) collective-permute-start(f32[264,128]{1,0:T(8,128)S(1)} %param.21), channel_id=1, source_target_pairs={{0,14},{2,12},{4,10},{6,8},{8,6},{10,4},{12,2},{14,0},{16,30},{18,... | collective-permute-start | bytes 405512 | tf_op jit(solution)/shard_map/cond/branch_6_fun/ppermute | solution.py:433
  14.5 5.9 %collective-permute-done.21 = f32[264,128]{1,0:T(8,128)} collective-permute-done((f32[264,128]{1,0:T(8,128)S(1)}, f32[264,128]{1,0:T(8,128)}, u32[]{:S(2)}, u32[]{:S(2)}) %collective-permute-start.21) | collective-permute-done | bytes 135200 | tf_op jit(solution)/shard_map/cond/branch_6_fun/ppermute | solution.py:433
  20.5 1.1 %collective-permute-done.45.refs_3_ = f32[648,128]{1,0:T(8,128)S(1)} collective-permute-done((f32[648,128]{1,0:T(8,128)S(1)}, f32[648,128]{1,0:T(8,128)S(1)}, u32[]{:S(2)}, u32[]{:S(2)}) %collective-permute-start.45) | collective-permute-done | bytes 331808 | tf_op jit(solution)/shard_map/ppermute | solution.py:433
  21.5 0.0 copy-done
  21.5 1.7 %stratum1_at0.1 = (f32[648,128]{1,0:T(8,128)S(1)}, f32[640,128]{1,0:T(8,128)S(1)}, f32[8,128]{1,0:T(8,128)S(1)}, bf16[256,128]{1,0:T(8,128)(2,1)S(1)}, f32[264,1...) custom-call(bf16[640,256]{1,0:T(8,128)(2,1)S(1)} %get-tuple-element., ...), custom_call_target="tpu_custom_call" | custom-call | flops 1 | bytes 1 | tf_op jit(solution)/shard_map/stratum1_at0/pallas_call | solution.py:335
  23.2 1.7 %collective-permute-start.47 = (f32[648,128]{1,0:T(8,128)S(1)}, f32[648,128]{1,0:T(8,128)S(1)}, u32[]{:S(2)}, u32[]{:S(2)}) collective-permute-start(f32[648,128]{1,0:T(8,128)S(1)} %get-tuple-element.315.refs_2_), channel_id=1, source_target_pairs={{0,1},{1,0},{2,3},{3,2},{4,5},{5,4},{6,7},{7,6},{8,9},{9,8},{10,11... | collective-permute-start | bytes 995336 | tf_op jit(solution)/shard_map/ppermute | solution.py:433
  24.9 3.7 %collective-permute-done.46.refs_3_ = f32[640,128]{1,0:T(8,128)S(1)} collective-permute-done((f32[640,128]{1,0:T(8,128)S(1)}, f32[640,128]{1,0:T(8,128)S(1)}, u32[]{:S(2)}, u32[]{:S(2)}) %collective-permute-start.46) | collective-permute-done | bytes 327712 | tf_op jit(solution)/shard_map/ppermute | solution.py:433
  28.5 1.0 %stratum1_at640.1 = (f32[640,128]{1,0:T(8,128)S(1)}, f32[640,128]{1,0:T(8,128)S(1)}, f32[264,128]{1,0:T(8,128)S(1)}, bf16[640,256]{1,0:T(8,128)(2,1)S(1)}) custom-call(bf16[640,256]{1,0:T(8,128)(2,1)S(1)} %get-tuple-element.306.refs_0_, bf16[3,1280,256]{2,1,0:T(8,128)(2,1)} %refs_1_.9, f32[640,128]{1,0:T(8,128)S(1)} %get-tuple-element.307.refs_2_, ...), custom_call_target="tpu_custom_call" | custom-call | flops 1 | bytes 1 | tf_op jit(solution)/shard_map/stratum1_at640/pallas_call | solution.py:335
  29.6 1.0 %collective-permute-start.48 = (f32[640,128]{1,0:T(8,128)S(1)}, f32[640,128]{1,0:T(8,128)S(1)}, u32[]{:S(2)}, u32[]{:S(2)}) collective-permute-start(f32[640,128]{1,0:T(8,128)S(1)} %get-tuple-element.320.refs_1_), channel_id=1, source_target_pairs={{0,1},{1,0},{2,3},{3,2},{4,5},{5,4},{6,7},{7,6},{8,9},{9,8},{10,11... | collective-permute-start | bytes 983048 | tf_op jit(solution)/shard_map/ppermute | solution.py:433
  30.5 8.5 %conditional.5 = (f32[264,128]{1,0:T(8,128)}) conditional(s32[]{:T(128)} %bitcast.2, f32[264,128]{1,0:T(8,128)S(1)} %get-tuple-element.318, f32[264,128]{1,0:T(8,128)S(1)} %get-tuple-element.318, f32[264,128]{1,0:T(8,128)S(1)} %get-tuple-element.318, f32[264,128]{1,0:T(8,128)S(1)} %get-tuple-element.318, ...), branch_computations={%region_30.0_spmd, %region_31.0_spmd, %region_32.0_spmd, %region_3... | conditional | bytes 540720 | solution.py:442
  30.5 5.3 %collective-permute-start.43 = (f32[264,128]{1,0:T(8,128)S(1)}, f32[264,128]{1,0:T(8,128)}, u32[]{:S(2)}, u32[]{:S(2)}) collective-permute-start(f32[264,128]{1,0:T(8,128)S(1)} %param.43), channel_id=1, source_target_pairs={{0,28},{2,30},{4,24},{6,26},{8,20},{10,22},{12,16},{14,18},{16,12}... | collective-permute-start | bytes 405512 | tf_op jit(solution)/shard_map/cond/branch_13_fun/ppermute | solution.py:433
  35.8 3.2 %collective-permute-done.43 = f32[264,128]{1,0:T(8,128)} collective-permute-done((f32[264,128]{1,0:T(8,128)S(1)}, f32[264,128]{1,0:T(8,128)}, u32[]{:S(2)}, u32[]{:S(2)}) %collective-permute-start.43) | collective-permute-done | bytes 135200 | tf_op jit(solution)/shard_map/cond/branch_13_fun/ppermute | solution.py:433
  39.0 0.0 collective-permute-done.47.refs_3_
  39.0 1.5 %stratum2_at0.1 = (f32[648,128]{1,0:T(8,128)S(1)}, f32[640,128]{1,0:T(8,128)S(1)}, f32[8,128]{1,0:T(8,128)S(1)}, bf16[256,128]{1,0:T(8,128)(2,1)S(1)}, f32[264,1...) custom-call(bf16[640,256]{1,0:T(8,128)(2,1)S(1)} %get-tuple-element., ...), custom_call_target="tpu_custom_call" | custom-call | flops 1 | bytes 1 | tf_op jit(solution)/shard_map/stratum2_at0/pallas_call | solution.py:335
  40.5 0.7 %collective-permute-start.51 = (f32[648,128]{1,0:T(8,128)S(1)}, f32[648,128]{1,0:T(8,128)S(1)}, u32[]{:S(2)}, u32[]{:S(2)}) collective-permute-start(f32[648,128]{1,0:T(8,128)S(1)} %get-tuple-element.331.refs_0_), channel_id=1, source_target_pairs={{0,1},{1,0},{2,3},{3,2},{4,5},{5,4},{6,7},{7,6},{8,9},{9,8},{10,11... | collective-permute-start | bytes 995336 | tf_op jit(solution)/shard_map/ppermute | solution.py:433
  41.2 1.5 %collective-permute-done.48.refs_2_ = f32[640,128]{1,0:T(8,128)S(1)} collective-permute-done((f32[640,128]{1,0:T(8,128)S(1)}, f32[640,128]{1,0:T(8,128)S(1)}, u32[]{:S(2)}, u32[]{:S(2)}) %collective-permute-start.48) | collective-permute-done | bytes 327712 | tf_op jit(solution)/shard_map/ppermute | solution.py:433
  42.7 1.0 %stratum2_at640.1 = (f32[320,128]{1,0:T(8,128)S(1)}, f32[320,128]{1,0:T(8,128)S(1)}, f32[640,128]{1,0:T(8,128)S(1)}, f32[264,128]{1,0:T(8,128)S(1)}) custom-call(bf16[640,256]{1,0:T(8,128)(2,1)S(1)} %get-tuple-element.319.refs_0_, f32[640,128]{1,0:T(8,128)S(1)} %get-tuple-element.320.refs_1_, f32[640,128]{1,0:T(8,128)S(1)} %collective-permute-done.48.refs_2_, ...), custom_call_target="tpu_custom_call" | custom-call | flops 1 | bytes 1 | tf_op jit(solution)/shard_map/stratum2_at640/pallas_call | solution.py:335
  43.7 1.0 %collective-permute-start.50 = (f32[320,128]{1,0:T(8,128)S(1)}, f32[320,128]{1,0:T(8,128)S(1)}, u32[]{:S(2)}, u32[]{:S(2)}) collective-permute-start(f32[320,128]{1,0:T(8,128)S(1)} %get-tuple-element.330.refs_0_), channel_id=1, source_target_pairs={{0,1},{1,0},{2,3},{3,2},{4,5},{5,4},{6,7},{7,6},{8,9},{9,8},{10,11... | collective-permute-start | bytes 491528 | tf_op jit(solution)/shard_map/ppermute | solution.py:433
  44.7 1.1 %collective-permute-start.49 = (f32[320,128]{1,0:T(8,128)S(1)}, f32[320,128]{1,0:T(8,128)S(1)}, u32[]{:S(2)}, u32[]{:S(2)}) collective-permute-start(f32[320,128]{1,0:T(8,128)S(1)} %get-tuple-element.328.refs_0_), channel_id=1, source_target_pairs={{0,1},{1,0},{2,3},{3,2},{4,5},{5,4},{6,7},{7,6},{8,9},{9,8},{10,11... | collective-permute-start | bytes 491528 | tf_op jit(solution)/shard_map/ppermute | solution.py:433
  45.8 0.0 collective-permute-start.52
  45.8 5.5 %collective-permute-done.51.refs_1_ = f32[648,128]{1,0:T(8,128)S(1)} collective-permute-done((f32[648,128]{1,0:T(8,128)S(1)}, f32[648,128]{1,0:T(8,128)S(1)}, u32[]{:S(2)}, u32[]{:S(2)}) %collective-permute-start.51) | collective-permute-done | bytes 331808 | tf_op jit(solution)/shard_map/ppermute | solution.py:433
  51.3 1.3 %user_log_at0.1 = (bf16[1280,128]{1,0:T(8,128)(2,1)}, f32[8,128]{1,0:T(8,128)S(1)}) custom-call(f32[648,128]{1,0:T(8,128)S(1)} %get-tuple-element.331.refs_0_, f32[648,128]{1,0:T(8,128)S(1)} %collective-permute-done.51.refs_1_, f32[640,128]{1,0:T(8,128)S(1)} %get-tuple-element.332.refs_2_, f32[8,128]{1,0:T(8,128)S(1)} %get-tuple-element.322.refs_4_.refs_3_), custom_call_target="tpu_custom_call" | custom-call | flops 3276800 | bytes 1146880 | tf_op jit(solution)/shard_map/user_log_at0/pallas_call | solution.py:390
  52.6 0.7 %collective-permute-done.50.refs_1_ = f32[320,128]{1,0:T(8,128)S(1)} collective-permute-done((f32[320,128]{1,0:T(8,128)S(1)}, f32[320,128]{1,0:T(8,128)S(1)}, u32[]{:S(2)}, u32[]{:S(2)}) %collective-permute-start.50) | collective-permute-done | bytes 163872 | tf_op jit(solution)/shard_map/ppermute | solution.py:433
  53.3 1.0 %user_log_at640.1 = (bf16[1280,128]{1,0:T(8,128)(2,1)}, f32[8,128]{1,0:T(8,128)S(1)}) custom-call(f32[320,128]{1,0:T(8,128)S(1)} %get-tuple-element.330.refs_0_, f32[320,128]{1,0:T(8,128)S(1)} %collective-permute-done.50.refs_1_, f32[640,128]{1,0:T(8,128)S(1)} %get-tuple-element.329.refs_2_, ...), custom_call_target="tpu_custom_call", output_to_operand_aliasing={{0}: (4, {})} | custom-call | flops 1638400 | bytes 573440 | tf_op jit(solution)/shard_map/user_log_at640/pallas_call | solution.py:390
  54.3 0.0 collective-permute-done.52.item
  54.3 0.9 %item_log.1 = bf16[256,128]{1,0:T(8,128)(2,1)} custom-call(f32[264,128]{1,0:T(8,128)S(1)} %collective-permute-done.52.item, f32[8,128]{1,0:T(8,128)S(1)} %get-tuple-element.335.refs_3_._), custom_call_target="tpu_custom_call" | custom-call | flops 1310720 | bytes 196608 | tf_op jit(solution)/shard_map/item_log/pallas_call | solution.py:420
  55.2 0.0 collective-permute-done.49.refs_1_
  55.2 1.0 %user_log_at960.1 = bf16[1280,128]{1,0:T(8,128)(2,1)} custom-call(f32[320,128]{1,0:T(8,128)S(1)} %get-tuple-element.328.refs_0_, f32[320,128]{1,0:T(8,128)S(1)} %collective-permute-done.49.refs_1_, f32[640,128]{1,0:T(8,128)S(1)} %get-tuple-element.329.refs_2_, f32[8,128]{1,0:T(8,128)S(1)} %get-tuple-element.335.refs_3_._, ...), custom_call_target="tpu_custom_call", output_to_operand_aliasing={{}: (4, {})} | custom-call | flops 1638400 | bytes 573440 | tf_op jit(solution)/shard_map/user_log_at960/pallas_call | solution.py:390
Async XLA Ops:
  1.6 7.6 %collective-permute-start.5 = (f32[256,128]{1,0:T(8,128)S(1)}, f32[256,128]{1,0:T(8,128)}, u32[]{:S(2)}, u32[]{:S(2)}) collective-permute-start(f32[256,128]{1,0:T(8,128)S(1)} %get-tuple-element.182), channel_id=1, source_target_pairs={{0,12},{2,14},{4,8},{6,10},{8,4},{10,6},{12,0},{14,2},{16,28},{18,... | collective-permute-start | bytes 393224 | tf_op jit(solution)/shard_map/cond/branch_5_fun/ppermute | solution.py:433
  10.7 10.8 %copy-start = (bf16[1280,128]{1,0:T(8,128)(2,1)S(1)}, bf16[1280,128]{1,0:T(8,128)(2,1)}, u32[]{:S(2)}) copy-start(bf16[1280,128]{1,0:T(8,128)(2,1)} %refs_4_.3) | copy-start | bytes 983044
  10.7 10.8 %collective-permute-start.45 = (f32[648,128]{1,0:T(8,128)S(1)}, f32[648,128]{1,0:T(8,128)S(1)}, u32[]{:S(2)}, u32[]{:S(2)}) collective-permute-start(f32[648,128]{1,0:T(8,128)S(1)} %get-tuple-element.303.refs_2_), channel_id=1, source_target_pairs={{0,1},{1,0},{2,3},{3,2},{4,5},{5,4},{6,7},{7,6},{8,9},{9,8},{10,11... | collective-permute-start | bytes 995336 | tf_op jit(solution)/shard_map/ppermute | solution.py:433
  13.4 15.2 %collective-permute-start.46 = (f32[640,128]{1,0:T(8,128)S(1)}, f32[640,128]{1,0:T(8,128)S(1)}, u32[]{:S(2)}, u32[]{:S(2)}) collective-permute-start(f32[640,128]{1,0:T(8,128)S(1)} %get-tuple-element.307.refs_2_), channel_id=1, source_target_pairs={{0,1},{1,0},{2,3},{3,2},{4,5},{5,4},{6,7},{7,6},{8,9},{9,8},{10,11... | collective-permute-start | bytes 983048 | tf_op jit(solution)/shard_map/ppermute | solution.py:433
  13.9 6.6 %collective-permute-start.21 = (f32[264,128]{1,0:T(8,128)S(1)}, f32[264,128]{1,0:T(8,128)}, u32[]{:S(2)}, u32[]{:S(2)}) collective-permute-start(f32[264,128]{1,0:T(8,128)S(1)} %param.21), channel_id=1, source_target_pairs={{0,14},{2,12},{4,10},{6,8},{8,6},{10,4},{12,2},{14,0},{16,30},{18,... | collective-permute-start | bytes 405512 | tf_op jit(solution)/shard_map/cond/branch_6_fun/ppermute | solution.py:433
  23.2 15.8 %collective-permute-start.47 = (f32[648,128]{1,0:T(8,128)S(1)}, f32[648,128]{1,0:T(8,128)S(1)}, u32[]{:S(2)}, u32[]{:S(2)}) collective-permute-start(f32[648,128]{1,0:T(8,128)S(1)} %get-tuple-element.315.refs_2_), channel_id=1, source_target_pairs={{0,1},{1,0},{2,3},{3,2},{4,5},{5,4},{6,7},{7,6},{8,9},{9,8},{10,11... | collective-permute-start | bytes 995336 | tf_op jit(solution)/shard_map/ppermute | solution.py:433
  29.6 13.1 %collective-permute-start.48 = (f32[640,128]{1,0:T(8,128)S(1)}, f32[640,128]{1,0:T(8,128)S(1)}, u32[]{:S(2)}, u32[]{:S(2)}) collective-permute-start(f32[640,128]{1,0:T(8,128)S(1)} %get-tuple-element.320.refs_1_), channel_id=1, source_target_pairs={{0,1},{1,0},{2,3},{3,2},{4,5},{5,4},{6,7},{7,6},{8,9},{9,8},{10,11... | collective-permute-start | bytes 983048 | tf_op jit(solution)/shard_map/ppermute | solution.py:433
  30.5 8.5 %collective-permute-start.43 = (f32[264,128]{1,0:T(8,128)S(1)}, f32[264,128]{1,0:T(8,128)}, u32[]{:S(2)}, u32[]{:S(2)}) collective-permute-start(f32[264,128]{1,0:T(8,128)S(1)} %param.43), channel_id=1, source_target_pairs={{0,28},{2,30},{4,24},{6,26},{8,20},{10,22},{12,16},{14,18},{16,12}... | collective-permute-start | bytes 405512 | tf_op jit(solution)/shard_map/cond/branch_13_fun/ppermute | solution.py:433
  40.5 10.8 %collective-permute-start.51 = (f32[648,128]{1,0:T(8,128)S(1)}, f32[648,128]{1,0:T(8,128)S(1)}, u32[]{:S(2)}, u32[]{:S(2)}) collective-permute-start(f32[648,128]{1,0:T(8,128)S(1)} %get-tuple-element.331.refs_0_), channel_id=1, source_target_pairs={{0,1},{1,0},{2,3},{3,2},{4,5},{5,4},{6,7},{7,6},{8,9},{9,8},{10,11... | collective-permute-start | bytes 995336 | tf_op jit(solution)/shard_map/ppermute | solution.py:433
  43.7 9.6 %collective-permute-start.50 = (f32[320,128]{1,0:T(8,128)S(1)}, f32[320,128]{1,0:T(8,128)S(1)}, u32[]{:S(2)}, u32[]{:S(2)}) collective-permute-start(f32[320,128]{1,0:T(8,128)S(1)} %get-tuple-element.330.refs_0_), channel_id=1, source_target_pairs={{0,1},{1,0},{2,3},{3,2},{4,5},{5,4},{6,7},{7,6},{8,9},{9,8},{10,11... | collective-permute-start | bytes 491528 | tf_op jit(solution)/shard_map/ppermute | solution.py:433
  44.7 10.6 %collective-permute-start.49 = (f32[320,128]{1,0:T(8,128)S(1)}, f32[320,128]{1,0:T(8,128)S(1)}, u32[]{:S(2)}, u32[]{:S(2)}) collective-permute-start(f32[320,128]{1,0:T(8,128)S(1)} %get-tuple-element.328.refs_0_), channel_id=1, source_target_pairs={{0,1},{1,0},{2,3},{3,2},{4,5},{5,4},{6,7},{7,6},{8,9},{9,8},{10,11... | collective-permute-start | bytes 491528 | tf_op jit(solution)/shard_map/ppermute | solution.py:433
  45.8 8.5 %collective-permute-start.52 = (f32[264,128]{1,0:T(8,128)S(1)}, f32[264,128]{1,0:T(8,128)S(1)}, u32[]{:S(2)}, u32[]{:S(2)}) collective-permute-start(f32[264,128]{1,0:T(8,128)S(1)} %get-tuple-element.337), channel_id=1, source_target_pairs={{0,30},{2,28},{4,26},{6,24},{8,22},{10,20},{12,18},{14,16},{16,14}... | collective-permute-start | bytes 405512 | tf_op jit(solution)/shard_map/ppermute | solution.py:433
